TPU v7x, 128 devices: a whole 4x4x4 slice. The times are simulated.
128 devices in a mesh: dp: 4 (over z), expert: 32 (over y, x, core).
Axes of the slice: x: 4, y: 4, z: 4, core: 2. Of those that a mesh axis runs over, the one named last changes fastest.
Arguments:
- tokens: bfloat16 [16384, 2048], P(('dp', 'expert')), may hold values from -6 to 6
- expert_ids: int32 [16384, 8], P(('dp', 'expert')), may hold values from 0 to 63, all different within a row; in each aligned block of 128 rows (0 to 127, 128 to 255, ...) at most 20 rows name the same one
- gate_scores: float32 [16384, 8], P(('dp', 'expert')), may hold values from 0.05 to 1
- w_in: bfloat16 [64, 2048, 1536], P('expert'), may hold values from -0.125 to 0.125
- w_out: bfloat16 [64, 768, 2048], P('expert'), may hold values from -0.21875 to 0.21875
- cotangent: bfloat16 [16384, 2048], P(('dp', 'expert')), may hold values from -6 to 6
Outputs:
- mixed: bfloat16 [16384, 2048], P(('dp', 'expert'))
- score_grad: float32 [16384, 8], P(('dp', 'expert'))
- grad_in: bfloat16 [64, 2048, 1536], P('expert', 'dp')
- grad_out: bfloat16 [64, 768, 2048], P('expert', None, 'dp')
Inputs may be any that keep to these rules, and one draw needn't show every extreme that they name: `expert_ids`: each token names 8 different experts. Among the 128 tokens of one device no expert is named by more than 20 tokens, and in some device's tokens an expert is named by exactly 20. Every expert is named by some token.
All inputs are finite; a program needn't handle non-finite values.
Results may differ from a plain program's by a relative error of at most 0.013.
Values may be sent and summed in bfloat16 or wider, within the bound.
A program may use at most 256 MiB of HBM per device.

v0:
```python
import jax
import jax.numpy as jnp
from jax import lax
from jax.sharding import PartitionSpec as P


def slot_plan(flat, experts, most):
    onehot = (flat[:, None] == jnp.arange(experts, dtype=jnp.int32)[None, :]).astype(jnp.int32)
    before = jnp.cumsum(onehot, axis=0) - onehot
    slot = jnp.sum(before * onehot, axis=1)
    place = flat * most + slot
    source = (
        jnp.full((experts * most,), -1, jnp.int32)
        .at[place]
        .set(jnp.arange(flat.shape[0], dtype=jnp.int32))
    )
    return (place, source)


def shards(tokens, expert_ids, gate_scores, w_in, w_out, cotangent):
    tok_rows, width = tokens.shape
    topk = expert_ids.shape[1]
    local_experts = w_in.shape[0]
    hidden_units = w_out.shape[1]
    peers = lax.axis_size("expert")
    experts = local_experts * peers
    most = 2 * max(1, 5 * tok_rows * topk // (8 * experts))
    splits = 1
    place, source = slot_plan(expert_ids.reshape(-1), experts, most)
    valid = source >= 0
    safe = jnp.maximum(source, 0)
    zero_bf = jnp.zeros((), jnp.bfloat16)
    rows_in = jnp.where(valid[:, None], tokens[safe // topk], zero_bf)
    send = rows_in.reshape(peers, local_experts, splits, most // splits, width)
    eff_in = w_in[:, None]
    eff_out = w_out[:, None]
    block = lax.all_to_all(send, "expert", split_axis=0, concat_axis=0, tiled=True)
    gate_up = jnp.einsum("nehmd,ehdf->nehmf", block, eff_in, preferred_element_type=jnp.float32)
    hidden = (jax.nn.silu(gate_up[..., :hidden_units]) * gate_up[..., hidden_units:]).astype(
        jnp.bfloat16
    )
    produced = jnp.einsum(
        "nehmf,ehfd->nehmd", hidden, eff_out, preferred_element_type=jnp.float32
    ).astype(jnp.bfloat16)
    returned = lax.all_to_all(produced, "expert", split_axis=0, concat_axis=0, tiled=True)
    back, received, gate_up, hidden = (returned, block, gate_up, hidden)
    returned_rows = back.reshape(experts * most, width)[place].reshape(tok_rows, topk, width)
    total = jnp.sum(gate_scores, axis=1, keepdims=True)
    weights = gate_scores / total
    mixed = jnp.sum(weights[:, :, None] * returned_rows.astype(jnp.float32), axis=1).astype(
        jnp.bfloat16
    )
    affinity = jnp.einsum(
        "tkd,td->tk", returned_rows, cotangent, preferred_element_type=jnp.float32
    )
    score_grad = (affinity - jnp.sum(weights * affinity, axis=1, keepdims=True)) / total
    scaled = (weights[:, :, None] * cotangent[:, None, :].astype(jnp.float32)).astype(jnp.bfloat16)
    scaled = scaled.reshape(tok_rows * topk, width)
    grad_send = jnp.where(valid[:, None], scaled[safe], zero_bf).reshape(
        peers, local_experts, splits, most // splits, width
    )
    grad_rows = lax.all_to_all(grad_send, "expert", split_axis=0, concat_axis=0, tiled=True)
    hidden_grad = jnp.einsum(
        "nehmd,ehfd->nehmf", grad_rows, eff_out, preferred_element_type=jnp.float32
    )
    gate = gate_up[..., :hidden_units]
    up = gate_up[..., hidden_units:]
    sig = jax.nn.sigmoid(gate)
    d_gate = hidden_grad * up * sig * (1.0 + gate * (1.0 - sig))
    d_up = hidden_grad * (gate * sig)
    gu_grad = jnp.concatenate([d_gate, d_up], axis=-1).astype(jnp.bfloat16)
    received = received.reshape(peers, local_experts, most, width)
    grad_rows = grad_rows.reshape(peers, local_experts, most, width)
    gu_grad = gu_grad.reshape(peers, local_experts, most, 2 * hidden_units)
    hidden = hidden.reshape(peers, local_experts, most, hidden_units)
    term_in = jnp.einsum("nemd,nemf->edf", received, gu_grad, preferred_element_type=jnp.float32)
    term_out = jnp.einsum("nemf,nemd->efd", hidden, grad_rows, preferred_element_type=jnp.float32)
    summed_in, summed_out = (
        lax.psum_scatter(
            term_in.astype(jnp.bfloat16), "dp", scatter_dimension=1, tiled=True
        ).astype(jnp.float32),
        lax.psum_scatter(
            term_out.astype(jnp.bfloat16), "dp", scatter_dimension=2, tiled=True
        ).astype(jnp.float32),
    )
    grad_in = summed_in.astype(jnp.bfloat16)
    grad_out = summed_out.astype(jnp.bfloat16)
    return (mixed, score_grad, grad_in, grad_out)


def solution(mesh):
    in_specs = (
        P(("dp", "expert"), None),
        P(("dp", "expert"), None),
        P(("dp", "expert"), None),
        P("expert", None, None),
        P("expert", None, None),
        P(("dp", "expert"), None),
    )
    out_specs = (
        P(("dp", "expert"), None),
        P(("dp", "expert"), None),
        P("expert", "dp", None),
        P("expert", None, "dp"),
    )
    return jax.shard_map(shards, mesh=mesh, in_specs=in_specs, out_specs=out_specs, check_vma=False)
```

profile of v0, /device:TPU:57, one launch (start us, length us, event | category | flops | bytes accessed | tf_op | source)
XLA Modules:
  0.0 589.0 jit_solution(3620914518156780338)
XLA Ops:
  7.2 0.7 broadcast_multiply_fusion
  7.9 0.8 copy.36
  8.9 0.1 copy.35
  9.0 0.1 mul.74
  9.1 18.0 %reduce-window.6 = s32[64,8,128]{2,1,0:T(8,128)S(1)} reduce-window(s32[64,8,128]{2,1,0:T(8,128)S(1)} %fusion.39, s32[]{:T(128)} %constant.34.clone.1), window={size=1x1x128 pad=0_0x0_0x127_0}, to_apply=%region_1.2 | reduce-window | flops 8323072 | bytes 524292 | tf_op jit(solution)/shard_map/reduce-window
  27.1 0.1 slice.24
  27.3 0.1 copy.38
  27.5 0.1 broadcast_add_fusion
  27.8 4.3 scatter_custom_fusion
  32.2 0.1 broadcast_in_dim.40
  32.3 0.6 pad_clamp_fusion
  32.9 6.2 %gather_fusion = bf16[1280,2048]{1,0:T(8,128)(2,1)} fusion(bf16[128,2048]{1,0:T(8,128)(2,1)S(1)} %copy-done, s32[2048]{0:T(1024)S(1)} %get-tuple-element.11), kind=kCustom, calls=%fused_computation | custom fusion | bytes 10490880 | tf_op jit(solution)/shard_map/gather | solution.py:33
  39.1 8.9 %gather.14 = bf16[32,2,1,20,2048]{4,3,1,0,2:T(8,128)(2,1)} reshape(bf16[1280,2048]{1,0:T(8,128)(2,1)} %gather_fusion) | data formatting | bytes 10485760 | tf_op jit(solution)/shard_map/gather | solution.py:33
  48.0 3.3 broadcast_select_fusion.1
  51.3 11.0 %copy.40 = bf16[32,2,1,20,2048]{4,1,3,2,0:T(2,128)(2,1)S(1)} copy(bf16[32,2,1,20,2048]{4,3,1,0,2:T(8,128)(2,1)S(1)} %broadcast_select_fusion.1) | data formatting | bytes 10485760 | tf_op jit(solution)/shard_map/jit(_where)/select_n | solution.py:33
  62.4 67.7 %all_to_all.15 = bf16[32,2,1,20,2048]{4,1,3,2,0:T(2,128)(2,1)S(1)} all-to-all(bf16[32,2,1,20,2048]{4,1,3,2,0:T(2,128)(2,1)S(1)} %copy.40), channel_id=1, replica_groups=mesh['dp'=4,'expert'=32] {'expert'}, dimensions={0} | all-to-all | bytes 10485760 | tf_op jit(solution)/shard_map/all_to_all | solution.py:37
  130.0 21.7 %fusion.11 = f32[32,2,1,20,1536]{4,0,3,1,2:T(8,128)S(1)} fusion(bf16[2,2048,1536]{2,1,0:T(8,128)(2,1)} %param.9, bf16[32,2,1,20,2048]{4,1,3,2,0:T(2,128)(2,1)S(1)} %all_to_all.15), kind=kOutput, calls=%fused_computation.22 | convolution fusion | flops 8053063680 | bytes 25690112 | tf_op jit(solution)/shard_map/nehmd,ehdf->nehmf/dot_general | solution.py:38
  151.8 3.1 copy-done.2
  154.8 1.2 fusion.32
  156.0 9.1 %convert_bitcast_fusion = bf16[32,2,1,20,2048]{4,0,3,1,2:T(8,128)(2,1)} fusion(bf16[32,2,20,768]{3,0,2,1:T(8,128)(2,1)S(1)} %fusion.32, bf16[2,768,2048]{2,1,0:T(8,128)(2,1)} %param.10), kind=kOutput, calls=%fused_computation.21 | convolution fusion | flops 4029153280 | bytes 13500416 | tf_op jit(solution)/shard_map/nehmf,ehfd->nehmd/dot_general | solution.py:42
  165.1 10.2 %copy.42 = bf16[32,2,1,20,2048]{4,1,3,2,0:T(2,128)(2,1)} copy(bf16[32,2,1,20,2048]{4,0,3,1,2:T(8,128)(2,1)} %convert_bitcast_fusion) | data formatting | bytes 10485760 | tf_op jit(solution)/shard_map/convert_element_type | solution.py:44
  175.3 7.2 %all-to-all-start.1 = ((bf16[32,2,1,20,2048]{4,1,3,2,0:T(2,128)(2,1)}), bf16[32,2,1,20,2048]{4,1,3,2,0:T(2,128)(2,1)}, u32[]{:S(2)}, u32[]{:S(2)}) async-start(bf16[32,2,1,20,2048]{4,1,3,2,0:T(2,128)(2,1)} %copy.42), calls=%async_computation.1 | async-start | bytes 10485760 | tf_op jit(solution)/shard_map/all_to_all | solution.py:45
  182.7 1.2 reduce_sum.38
  183.9 1.3 broadcast_clamp_fusion
  185.2 57.6 %all-to-all-done.1 = bf16[32,2,1,20,2048]{4,1,3,2,0:T(2,128)(2,1)} async-done(((bf16[32,2,1,20,2048]{4,1,3,2,0:T(2,128)(2,1)}), bf16[32,2,1,20,2048]{4,1,3,2,0:T(2,128)(2,1)}, u32[]{:S(2)}, u32[]{:S(2)}) %all-to-all-start.1) | async-done | bytes 5242912 | tf_op jit(solution)/shard_map/all_to_all | solution.py:45
  242.8 7.9 %copy.43 = bf16[32,2,1,20,2048]{4,3,1,0,2:T(8,128)(2,1)} copy(bf16[32,2,1,20,2048]{4,1,3,2,0:T(2,128)(2,1)} %all-to-all-done.1) | data formatting | bytes 10485760 | tf_op jit(solution)/shard_map/all_to_all | solution.py:45
  250.7 9.4 %reshape.143 = bf16[1280,2048]{1,0:T(8,128)(2,1)} reshape(bf16[32,2,1,20,2048]{4,3,1,0,2:T(8,128)(2,1)} %copy.43) | data formatting | bytes 10485760 | tf_op jit(solution)/shard_map/reshape | solution.py:47
  260.1 12.1 %gather_fusion.1 = bf16[1024,2048]{1,0:T(8,128)(2,1)} fusion(bf16[1280,2048]{1,0:T(8,128)(2,1)} %reshape.143, s32[1024]{0:T(1024)} %broadcast_clamp_fusion), kind=kCustom, calls=%fused_computation.1 | custom fusion | bytes 8392704 | tf_op jit(solution)/shard_map/gather | solution.py:47
  272.1 5.5 fusion.20
  277.7 0.9 copy.50
  278.6 1.3 fusion.41
  279.9 0.1 copy.34
  280.1 2.5 fusion.2
  282.6 13.6 %gather_fusion.2 = bf16[1280,2048]{1,0:T(8,128)(2,1)} fusion(bf16[1024,2048]{1,0:T(8,128)(2,1)} %fusion.2, s32[2048]{0:T(1024)S(1)} %copy-done.10), kind=kCustom, calls=%fused_computation.2 | custom fusion | bytes 10490880 | tf_op jit(solution)/shard_map/gather | solution.py:59
  296.1 8.9 %gather.17 = bf16[32,2,1,20,2048]{4,3,1,0,2:T(8,128)(2,1)} reshape(bf16[1280,2048]{1,0:T(8,128)(2,1)} %gather_fusion.2) | data formatting | bytes 10485760 | tf_op jit(solution)/shard_map/gather | solution.py:59
  305.0 3.3 broadcast_select_fusion
  308.3 11.0 %copy.45 = bf16[32,2,1,20,2048]{4,1,3,2,0:T(2,128)(2,1)S(1)} copy(bf16[32,2,1,20,2048]{4,3,1,0,2:T(8,128)(2,1)S(1)} %broadcast_select_fusion) | data formatting | bytes 10485760 | tf_op jit(solution)/shard_map/jit(_where)/select_n | solution.py:59
  319.4 68.2 %all_to_all.16 = bf16[32,2,1,20,2048]{4,1,3,2,0:T(2,128)(2,1)S(1)} all-to-all(bf16[32,2,1,20,2048]{4,1,3,2,0:T(2,128)(2,1)S(1)} %copy.45), channel_id=1, replica_groups=mesh['dp'=4,'expert'=32] {'expert'}, dimensions={0} | all-to-all | bytes 10485760 | tf_op jit(solution)/shard_map/all_to_all | solution.py:62
  387.6 2.3 copy-done.4
  389.9 10.3 %bitcast_convert_fusion.1 = bf16[2,768,2048]{2,1,0:T(8,128)(2,1)} fusion(bf16[32,2,20,768]{3,0,2,1:T(8,128)(2,1)S(1)} %fusion.32, bf16[32,2,1,20,2048]{4,1,3,2,0:T(2,128)(2,1)S(1)} %all_to_all.16), kind=kOutput, calls=%fused_computation.7 | convolution fusion | flops 4029677568 | bytes 13500416 | tf_op jit(solution)/shard_map/nemf,nemd->efd/dot_general | solution.py:77
  400.2 0.2 reduce-scatter.3.cloned.1.call-start
  400.5 15.5 %fusion.34 = (bf16[32,2,20,768]{3,0,2,1:T(8,128)(2,1)S(1)}, bf16[32,2,20,768]{3,0,2,1:T(8,128)(2,1)S(1)}) fusion(f32[32,2,1,20,1536]{4,0,3,1,2:T(8,128)} %copy-done.2, bf16[2,768,2048]{2,1,0:T(8,128)(2,1)} %param.10, bf16[32,2,1,20,2048]{4,1,3,2,0:T(2,128)(2,1)} %copy-done.4), kind=kOutput, calls=%fused_computation.43 | convolution fusion | flops 4039311360 | bytes 23330816 | tf_op jit(solution)/shard_map/nehmd,ehfd->nehmf/dot_general | solution.py:63
  416.0 35.2 %bitcast_convert_fusion = bf16[2,2048,1536]{2,1,0:T(8,128)(2,1)} fusion(bf16[32,2,1,20,2048]{4,1,3,2,0:T(2,128)(2,1)} %copy-done.3, bf16[32,2,20,768]{3,0,2,1:T(8,128)(2,1)S(1)} %get-tuple-element.7, bf16[32,2,20,768]{3,0,2,1:T(8,128)(2,1)S(1)} %get-tuple-element.6), kind=kOutput, calls=%fused_computation.4 | convolution fusion | flops 8067219456 | bytes 21757952 | tf_op jit(solution)/shard_map/nemd,nemf->edf/dot_general | solution.py:76
  451.3 0.6 copy-done.9
  451.9 0.6 fusion.42
  452.5 7.3 %multiply_reduce_fusion = bf16[128,2048]{1,0:T(8,128)(2,1)} fusion(bf16[1024,2048]{1,0:T(8,128)(2,1)} %gather_fusion.1, f32[128,8]{1,0:T(8,128)S(1)} %copy-done.6), kind=kLoop, calls=%fused_computation.10 | loop fusion | flops 6029312 | bytes 4722688 | tf_op jit(solution)/shard_map/reduce_sum | solution.py:50
  459.8 4.7 reduce-scatter.5.cloned.1.call-done
  464.5 117.4 %reduce-scatter.3.cloned.1.call-done = bf16[2,512,1536]{2,1,0:T(8,128)(2,1)} async-done(((bf16[2,2048,1536]{2,1,0:T(8,128)(2,1)}), bf16[2,512,1536]{2,1,0:T(8,128)(2,1)}) %reduce-scatter.3.cloned.1.call-update) | async-done | bytes 3145744 | tf_op jit(solution)/shard_map/reduce_scatter | solution.py:79
  (41 shorter events, 0.7 us)
Async XLA Ops:
  7.2 25.7 %copy-start = (bf16[128,2048]{1,0:T(8,128)(2,1)S(1)}, bf16[128,2048]{1,0:T(8,128)(2,1)}, u32[]{:S(2)}) copy-start(bf16[128,2048]{1,0:T(8,128)(2,1)} %param.6) | copy-start | bytes 1572868
  27.8 4.3 copy-start.11
  130.0 21.7 %copy-start.3 = (bf16[32,2,1,20,2048]{4,1,3,2,0:T(2,128)(2,1)}, bf16[32,2,1,20,2048]{4,1,3,2,0:T(2,128)(2,1)S(1)}, u32[]{:S(2)}) copy-start(bf16[32,2,1,20,2048]{4,1,3,2,0:T(2,128)(2,1)S(1)} %all_to_all.15) | copy-start | bytes 15728644
  151.7 3.1 copy-start.2
  175.3 7.3 %copy-start.7 = (bf16[128,2048]{1,0:T(8,128)(2,1)S(1)}, bf16[128,2048]{1,0:T(8,128)(2,1)}, u32[]{:S(2)}) copy-start(bf16[128,2048]{1,0:T(8,128)(2,1)} %param.11) | copy-start | bytes 1572868
  175.3 67.5 %all-to-all-start.1 = ((bf16[32,2,1,20,2048]{4,1,3,2,0:T(2,128)(2,1)}), bf16[32,2,1,20,2048]{4,1,3,2,0:T(2,128)(2,1)}, u32[]{:S(2)}, u32[]{:S(2)}) async-start(bf16[32,2,1,20,2048]{4,1,3,2,0:T(2,128)(2,1)} %copy.42), calls=%async_computation.1 | async-start | bytes 10485760 | tf_op jit(solution)/shard_map/all_to_all | solution.py:45
  182.5 282.0 %reduce-scatter.5.cloned.1.call-start = ((), (), s32[]{:S(2)}) async-start(), calls=%async_computation.6 | async-start | bytes 7864320 | tf_op jit(solution)/shard_map/reduce_scatter | solution.py:82
  277.7 4.9 copy-start.10
  278.6 1.3 copy-start.8
  280.0 16.1 %copy-start.5 = (f32[128,8]{1,0:T(8,128)}, f32[128,8]{1,0:T(8,128)S(1)}, u32[]{:S(2)}) copy-start(f32[128,8]{1,0:T(8,128)S(1)} %copy.34) | copy-start | bytes 12292
  387.6 2.3 copy-start.4
  400.2 181.7 %reduce-scatter.3.cloned.1.call-start = ((), (), s32[]{:S(2)}) async-start(), calls=%async_computation.5 | async-start | bytes 15728640 | tf_op jit(solution)/shard_map/reduce_scatter | solution.py:79
  451.2 0.7 copy-start.9
  451.2 0.7 copy-start.12
  451.2 0.7 copy-start.13
  451.3 1.3 copy-start.6
  451.3 130.6 %copy-start.1 = (bf16[128,2048]{1,0:T(8,128)(2,1)S(1)}, bf16[128,2048]{1,0:T(8,128)(2,1)}, u32[]{:S(2)}) copy-start(bf16[128,2048]{1,0:T(8,128)(2,1)} %param.6) | copy-start | bytes 1572868
Sparse Core Ops, SparseCore 0:
  400.4 64.1 reduce-scatter.4
  467.6 114.2 reduce-scatter.2
where the time goes:
time: 597 us; the launch traced here: 589 us
  waiting for transfers between devices  180 us (30%)
  blocking collectives  136 us (23%)
  local copies, waits for them, and re-layouts  112 us (19%)
  matrix products  97.3 us (16%)
  other arithmetic  41.8 us (7%)
  between operations  14.6 us (2%)
  starting transfers between devices  7.47 us (1%)
    reduce_scatter x1, waiting for transfers between devices, shards(): lax.psum_scatter(term_in.astype(jnp.bfloat16), 'dp', scatter_dimension=1,...  117 us
    all_to_all x1, blocking collectives, shards(): lax.all_to_all(grad_send, 'expert', split_axis=0, concat_axis=0, tiled=True)  68.2 us
    all_to_all x1, blocking collectives, shards(): lax.all_to_all(send, 'expert', split_axis=0, concat_axis=0, tiled=True)  67.7 us
    all_to_all x1, waiting for transfers between devices, shards(): lax.all_to_all(produced, 'expert', split_axis=0, concat_axis=0, tiled=True)  57.6 us
    dot_general x1, matrix products, shards(): jnp.einsum('nemd,nemf->edf', received, gu_grad, preferred_element_type=jn...  35.2 us
    gather x2, local copies, waits for them, and re-layouts, shards(): scaled[safe]  22.5 us
    dot_general x1, matrix products, shards(): jnp.einsum('nehmd,ehdf->nehmf', block, eff_in, preferred_element_type=jnp...  21.7 us
    another operation x4, other arithmetic  19.4 us
  transfers between devices with their start and end apart: 3, of which 3 were waited for; matrix products, arithmetic and copies ran while one was open for 10% of the time, Pallas kernels for 0%

commit v1 on v0

v1 whole, which is shorter than its diff:
```python
import functools

import jax
import jax.numpy as jnp
from jax import lax
from jax.experimental import pallas as pl
from jax.experimental.pallas import tpu as pltpu
from jax.sharding import PartitionSpec as P

MESH = pl.DeviceIdType.MESH
BF = jnp.bfloat16
F32 = jnp.float32

TOK = 128
D = 2048
FF = 768
PEERS = 32
MAIN = 16
GRP = 512
BLK = 80
ROWS = PEERS * 20
AREA = PEERS * BLK
UROWS = 384 + 3 * 256
BATCH = 16


def dot(a, b, dims=((1,), (0,))):
    return lax.dot_general(a, b, (dims, ((), ())), preferred_element_type=F32)


def peer(me, i):
    c = lax.rem(me, 2)
    x = lax.rem(lax.div(me, 2), 4)
    y = lax.div(me, 8)
    dc = lax.rem(i, 2)
    dx = lax.rem(lax.div(i, 2), 4)
    dy = lax.div(i, 8)
    return lax.rem(y + dy, 4) * 8 + lax.rem(x + dx, 4) * 2 + lax.rem(c + dc, 2)


def turn(me, i):
    return peer(me, lax.rem(i * 11, PEERS))


def iota(shape, dim):
    return lax.broadcasted_iota(jnp.int32, shape, dim)


def rows_of(p):
    if isinstance(p, int):
        return (0, 384) if p == 0 else (384 + 256 * (p - 1), 256)
    return (pl.multiple_of(384 + 256 * (p - 1), 128), 256)


def kernel(
    tok, cot, ids, scores, win_hbm, wout_hbm,
    mixed, score, gin, gout, back, parts,
    big, recv, win, wout, xs, xt, ht, hid, gate, up, gg, stage, slot, wgt, cut, perm, perm_t,
    over, side, slot4, wgt4, aff, macc,
    d_send, d_recv, r_send, r_recv, z_send, z_recv, l_sem, w_sem, o_sem,
):
    b = lax.axis_index("dp")
    me = lax.axis_index("expert")
    right = lax.rem(b + 1, 4)
    left = lax.rem(b + 3, 4)

    def load_in(j):
        return pltpu.make_async_copy(win_hbm.at[j], win, w_sem.at[0])

    def load_out(j):
        return pltpu.make_async_copy(wout_hbm.at[j], wout, w_sem.at[1])

    load_in(0).start()
    load_out(0).start()

    barrier = pltpu.get_barrier_semaphore()

    def greet(i, _):
        pl.semaphore_signal(barrier, inc=1, device_id=(b, peer(me, i)), device_id_type=MESH)
        return 0

    lax.fori_loop(1, PEERS, greet, 0)
    pl.semaphore_signal(barrier, inc=1, device_id=(right, me), device_id_type=MESH)
    pl.semaphore_signal(barrier, inc=1, device_id=(left, me), device_id_type=MESH)

    names = ids[...]
    total = jnp.sum(scores[...], axis=0, keepdims=True)
    weights = scores[...] / total
    row = iota((64, TOK), 0)
    expert = 2 * lax.rem(row, PEERS) + lax.div(row, PEERS)
    member = jnp.zeros((64, TOK), F32)
    weight = jnp.zeros((64, TOK), F32)
    for k in range(8):
        hit = names[k : k + 1, :] == expert
        member = member + jnp.where(hit, 1.0, 0.0)
        weight = weight + jnp.where(hit, weights[k : k + 1, :], 0.0)
    earlier = jnp.where(iota((TOK, TOK), 0) < iota((TOK, TOK), 1), 1.0, 0.0).astype(BF)
    slot[...] = jnp.where(member > 0.0, dot(member.astype(BF), earlier), -1.0)
    wgt[...] = weight

    r0, r1 = iota((GRP, GRP), 0), iota((GRP, GRP), 1)

    def place(m):
        r = lax.rem(m, 128)
        return 16 * lax.div(r, 4) + 4 * lax.div(m, 128) + lax.rem(r, 4)

    perm[...] = jnp.where(r1 == place(r0), 1.0, 0.0).astype(BF)
    perm_t[...] = jnp.where(r0 == place(r1), 1.0, 0.0).astype(BF)

    main_slot = iota((MAIN, TOK), 0).astype(F32)
    over_row = iota((MAIN, TOK), 0)
    over_slot = (16 + lax.rem(over_row, 4)).astype(F32)
    over_group = lax.div(over_row, 4)

    def block(q):
        return pl.ds(pl.multiple_of(q * BLK, 16), BLK)

    def send_block(j, a, q):
        return big.at[j, pl.ds(pl.multiple_of(a * AREA + q * BLK, 16), BLK)]

    def dispatch_copy(j, a, q, lands):
        return pltpu.make_async_remote_copy(
            src_ref=send_block(j, a, q),
            dst_ref=recv.at[2 * j + a, block(lands)],
            send_sem=d_send.at[2 * j + a, q],
            recv_sem=d_recv.at[2 * j + a, lands],
            device_id=(b, q),
            device_id_type=MESH,
        )

    def own_copy(j, a):
        return pltpu.make_async_copy(
            send_block(j, a, me), recv.at[2 * j + a, block(me)], l_sem.at[2 * j + a]
        )

    def dispatch(j, a):
        source = (tok, cot)[a]

        def batch(g, _):
            hots, overs, w_main, w_over = [], [], [], []
            for u in range(BATCH):
                q = turn(me, g * BATCH + u)
                mine = slot[pl.ds(j * PEERS + q, 1), :]
                hot = jnp.where(main_slot == mine, 1.0, 0.0)
                hot4 = jnp.where(over_slot == mine, 1.0, 0.0)
                hots.append(hot)
                overs.append(
                    jnp.concatenate(
                        [jnp.where(over_group == c, hot4, 0.0) for c in range(4)], axis=1
                    )
                )
                if a == 1:
                    heavy = wgt[pl.ds(j * PEERS + q, 1), :]
                    w_main.append(jnp.sum(hot * heavy, axis=1, keepdims=True))
                    w_over.append(jnp.sum(hot4 * heavy, axis=1, keepdims=True))
            pick = jnp.concatenate(hots, axis=0).astype(BF)
            pick4 = jnp.concatenate(overs, axis=0).astype(BF)
            scale = jnp.concatenate(w_main, axis=0) if a == 1 else None
            scale4 = jnp.concatenate(w_over, axis=0) if a == 1 else None
            extra = None
            for c in range(4):
                columns = source[:, c * GRP : (c + 1) * GRP]
                rows = dot(pick, columns)
                more = dot(pick4[:, c * TOK : (c + 1) * TOK], columns)
                extra = more if extra is None else extra + more
                if a == 1:
                    rows = rows * scale
                rows = rows.astype(BF)
                for u in range(BATCH):
                    q = turn(me, g * BATCH + u)
                    at = pl.multiple_of(a * AREA + q * BLK + 16 * c, 16)
                    big[j, pl.ds(at, 16), :] = rows[u * 16 : u * 16 + 16, :]
            if a == 1:
                extra = extra * scale4
            extra = extra.astype(BF)
            for u in range(BATCH):
                q = turn(me, g * BATCH + u)
                at = pl.multiple_of(a * AREA + q * BLK + 64, 16)
                big[j, pl.ds(at, 16), :] = extra[u * 16 : u * 16 + 16, :]

            def go(i, _):
                q = turn(me, i)

                @pl.when(i > 0)
                def _():
                    dispatch_copy(j, a, q, me).start()

                @pl.when(i == 0)
                def _():
                    own_copy(j, a).start()

                return 0

            lax.fori_loop(g * BATCH, (g + 1) * BATCH, go, 0)
            return 0

        lax.fori_loop(0, PEERS // BATCH, batch, 0)

    def assemble(aj, wait):
        def one(i, _):
            q = turn(me, i)
            if wait is not None:
                wait(i, q)
            for c in range(4):
                xs[pl.ds(pl.multiple_of(q * 16, 16), 16), c * GRP : (c + 1) * GRP] = recv[
                    aj, pl.ds(pl.multiple_of(q * BLK + 16 * c, 16), 16), :
                ]
            over[pl.ds(pl.multiple_of(q * 16, 16), 16), :] = recv[
                aj, pl.ds(pl.multiple_of(q * BLK + 64, 16), 16), :
            ]
            return 0

        lax.fori_loop(0, PEERS, one, 0)
        moved = dot(perm[...], over[...]).astype(BF)
        for c in range(4):
            xs[512:640, c * GRP : (c + 1) * GRP] = moved[c * 128 : (c + 1) * 128, :]

    def arrive(j, a):
        def wait(i, q):
            @pl.when(i > 0)
            def _():
                dispatch_copy(j, a, q, q).wait_recv()

            @pl.when(i == 0)
            def _():
                own_copy(j, a).wait()

        assemble(2 * j + a, wait)

    def return_copy(j, q, lands):
        return pltpu.make_async_remote_copy(
            src_ref=recv.at[2 * j, block(q)],
            dst_ref=back.at[j, block(lands)],
            send_sem=r_send.at[j, q],
            recv_sem=r_recv.at[j, lands],
            device_id=(b, q),
            device_id_type=MESH,
        )

    def own_return(j):
        return pltpu.make_async_copy(recv.at[2 * j, block(me)], back.at[j, block(me)], l_sem.at[4 + j])

    def forward(j):
        arrive(j, 0)

        def flip(c, _):
            at = pl.ds(pl.multiple_of(c * GRP, GRP), GRP)
            xt[at, :] = xs[:, at].T
            return 0

        lax.fori_loop(0, 4, flip, 0)
        load_in(j).wait()

        def part(n, _):
            at = pl.ds(pl.multiple_of(n * 256, 256), 256)
            g = dot(xs[...], win[:, at])
            u = dot(xs[...], win[:, pl.ds(pl.multiple_of(FF + n * 256, 256), 256)])
            gate[:, at] = g
            up[:, at] = u
            h = (g * jax.nn.sigmoid(g) * u).astype(BF)
            hid[:, at] = h
            ht[at, :] = h.T
            return 0

        lax.fori_loop(0, FF // 256, part, 0)
        if j == 0:
            load_in(1).start()
        load_out(j).wait()

        def produce(c, _):
            made = dot(hid[...], wout[:, pl.ds(pl.multiple_of(c * GRP, GRP), GRP)]).astype(BF)
            for q in range(PEERS):
                recv[2 * j, pl.ds(pl.multiple_of(q * BLK + 16 * c, 16), 16), :] = made[
                    16 * q : 16 * q + 16, :
                ]
            side[pl.ds(pl.multiple_of(c * 128, 128), 128), :] = made[512:640, :]
            return 0

        lax.fori_loop(0, 4, produce, 0)
        moved = dot(perm_t[...], side[...]).astype(BF)
        for q in range(PEERS):
            recv[2 * j, q * BLK + 64 : q * BLK + 80, :] = moved[16 * q : 16 * q + 16, :]

        def go(i, _):
            return_copy(j, turn(me, i), me).start()
            return 0

        lax.fori_loop(1, PEERS, go, 0)
        own_return(j).start()

    def unit_rows(u, p):
        at, n = rows_of(p)
        return pl.ds(pl.multiple_of(u * UROWS + at, 128), n)

    def z_copy(j, k, p):
        side_of = lax.rem(jnp.int32(k), 2) if isinstance(k, int) else lax.rem(k, 2)
        to = jnp.where(side_of == 0, right, left)
        return pltpu.make_async_remote_copy(
            src_ref=big.at[j, unit_rows(k, p)],
            dst_ref=parts.at[j, unit_rows(k, p)],
            send_sem=z_send.at[j, k, p],
            recv_sem=z_recv.at[j, k, p],
            device_id=(to, me),
            device_id_type=MESH,
        )

    def unit_of(u):
        odd = lax.rem(u, 2)
        far = jnp.where(u < 2, 2, jnp.where(u < 6, 1 + 2 * odd, 0))
        half = jnp.where(lax.div(u, 2) == 1, 1 - odd, odd)
        return lax.rem(b + far, 4), half

    def backward(j):
        arrive(j, 1)

        def sent(i, _):
            q = turn(me, i)
            dispatch_copy(j, 0, q, me).wait_send()
            dispatch_copy(j, 1, q, me).wait_send()
            return 0

        lax.fori_loop(1, PEERS, sent, 0)

        def unit_out(u, _):
            o, half = unit_of(u)
            term = dot(
                ht[pl.ds(pl.multiple_of(half * 384, 128), 384), :],
                xs[:, pl.ds(pl.multiple_of(o * GRP, GRP), GRP)],
            )
            big[j, unit_rows(u, 0), :] = term.astype(BF)

            @pl.when(u < 4)
            def _():
                z_copy(j, u, 0).start()

            return 0

        lax.fori_loop(0, 8, unit_out, 0)

        def part(n, _):
            at = pl.ds(pl.multiple_of(n * 256, 256), 256)
            grad = dot(xs[...], wout[at, :], ((1,), (1,)))
            g = gate[:, at]
            s = jax.nn.sigmoid(g)
            gg[:, at] = (grad * up[:, at] * s * (1.0 + g * (1.0 - s))).astype(BF)
            gg[:, pl.ds(pl.multiple_of(FF + n * 256, 256), 256)] = (grad * (g * s)).astype(BF)
            return 0

        lax.fori_loop(0, FF // 256, part, 0)
        if j == 0:
            load_out(1).start()

        def unit_in(i, _):
            p = 1 + lax.div(i, 8)
            u = lax.rem(i, 8)
            o, half = unit_of(u)
            term = dot(
                xt[pl.ds(pl.multiple_of(o * GRP + half * 256, 256), 256), :],
                gg[:, pl.ds(pl.multiple_of((p - 1) * GRP, GRP), GRP)],
            )
            big[j, unit_rows(u, p), :] = term.astype(BF)

            @pl.when(u < 4)
            def _():
                z_copy(j, u, p).start()

            return 0

        lax.fori_loop(0, 24, unit_in, 0)

    def fetch(j, k, p, where):
        n = rows_of(p)[1]
        return pltpu.make_async_copy(
            parts.at[j, unit_rows(k, p)], stage.at[where, pl.ds(0, n)], o_sem.at[where]
        )

    def middle(j, p):
        n = rows_of(p)[1]
        for d in range(2):
            z_copy(j, d, p).wait_recv()
            fetch(j, d, p, d).start()
        for d in range(2):
            fetch(j, d, p, d).wait()
            at = unit_rows(4 + d, p)
            both = big[j, at, :].astype(F32) + stage[d, 0:n, :].astype(F32)
            big[j, at, :] = both.astype(BF)
            z_copy(j, 4 + d, p).start()

    def result_copy(j, h, p):
        at, n = rows_of(p)
        if isinstance(p, int) and p == 0:
            to = gout.at[j, pl.ds(384 * h, 384)]
        else:
            to = gin.at[j, pl.ds(256 * h, 256), pl.ds(pl.multiple_of((p - 1) * GRP, GRP), GRP)]
        return pltpu.make_async_copy(big.at[j, unit_rows(6 + h, p)], to, o_sem.at[4 + h])

    def finish(j, p):
        n = rows_of(p)[1]
        for k in (3, 2, 4, 5):
            z_copy(j, k, p).wait_recv()
            fetch(j, k, p, k - 2).start()
        for h in range(2):
            fetch(j, 4 + h, p, 2 + h).wait()
            fetch(j, 3 - h, p, 1 - h).wait()
            at = unit_rows(6 + h, p)
            whole = (
                big[j, at, :].astype(F32)
                + stage[2 + h, 0:n, :].astype(F32)
                + stage[1 - h, 0:n, :].astype(F32)
            )
            big[j, at, :] = whole.astype(BF)
            result_copy(j, h, p).start()
        for h in range(2):
            result_copy(j, h, p).wait()

    def each(fn, j, lo, hi):
        if lo == 0:
            fn(j, 0)

        def one(p, _):
            fn(j, p)
            return 0

        lax.fori_loop(max(lo, 1), hi, one, 0)

    def combine(j):
        def arrived(i, _):
            q = turn(me, i)
            return_copy(j, q, q).wait_recv()
            return_copy(j, q, q).wait_send()
            return 0

        lax.fori_loop(1, PEERS, arrived, 0)
        own_return(j).wait()
        whole = pltpu.make_async_copy(back.at[j], recv.at[2 * j + 1], l_sem.at[6])
        whole.start()
        whole.wait()
        assemble(2 * j + 1, None)
        mine = slot[j * PEERS : (j + 1) * PEERS, :]
        heavy = wgt[j * PEERS : (j + 1) * PEERS, :]
        for s in range(4):
            slot4[pl.ds(s, PEERS, stride=4), :] = mine
            wgt4[pl.ds(s, PEERS, stride=4), :] = heavy
        sub = iota((PEERS, MAIN, TOK), 1).astype(F32)
        hot = jnp.where(jnp.broadcast_to(mine[:, None, :], (PEERS, MAIN, TOK)) == sub, 1.0, 0.0)
        hot_w = (hot * heavy[:, None, :]).reshape(512, TOK)
        hot = hot.reshape(512, TOK)
        tail = (16 + lax.rem(iota((128, TOK), 0), 4)).astype(F32)
        hot4 = jnp.where(slot4[...] == tail, 1.0, 0.0)
        hot4_w = hot4 * wgt4[...]
        dots = dot(xs[...], cot[...], ((1,), (1,)))
        near = jnp.sum((dots[0:512, :] * hot).reshape(PEERS, MAIN, TOK), axis=1)
        slot4[...] = dots[512:640, :] * hot4
        for s in range(4):
            near = near + slot4[pl.ds(s, PEERS, stride=4), :]
        aff[j * PEERS : (j + 1) * PEERS, :] = near
        mix_t = jnp.concatenate([hot_w.T, hot4_w.T], axis=1).astype(BF)
        for c in range(4):
            at = slice(c * GRP, (c + 1) * GRP)
            made = dot(mix_t, xs[:, at])
            if j == 0:
                macc[:, at] = made
            else:
                mixed[:, at] = (macc[:, at] + made).astype(BF)

    pl.semaphore_wait(barrier, PEERS + 1)
    dispatch(0, 0)
    dispatch(0, 1)
    dispatch(1, 0)
    dispatch(1, 1)
    forward(0)
    backward(0)
    each(middle, 0, 0, 2)
    forward(1)
    each(middle, 0, 2, 4)
    backward(1)
    each(finish, 0, 0, 4)
    each(middle, 1, 0, 4)
    combine(0)
    combine(1)
    found = []
    for k in range(8):
        found.append(
            jnp.sum(jnp.where(ids[k : k + 1, :] == expert, aff[...], 0.0), axis=0, keepdims=True)
        )
    affinity = jnp.concatenate(found, axis=0)
    score[...] = (affinity - jnp.sum(weights * affinity, axis=0, keepdims=True)) / total
    each(finish, 1, 0, 4)

    def sent(j, p):
        for k in range(6):
            z_copy(j, k, p).wait_send()

    each(sent, 0, 0, 4)
    each(sent, 1, 0, 4)


def shards(tokens, expert_ids, gate_scores, w_in, w_out, cotangent):
    vm = pl.BlockSpec(memory_space=pltpu.VMEM)
    anywhere = pl.BlockSpec(memory_space=pl.ANY)
    mixed, score_t, grad_in, grad_out, _, _ = pl.pallas_call(
        kernel,
        out_shape=[
            jax.ShapeDtypeStruct((TOK, D), BF),
            jax.ShapeDtypeStruct((8, TOK), F32),
            jax.ShapeDtypeStruct((2, 512, 2 * FF), BF),
            jax.ShapeDtypeStruct((2, FF, 512), BF),
            jax.ShapeDtypeStruct((2, AREA, GRP), BF),
            jax.ShapeDtypeStruct((2, 6 * UROWS, GRP), BF),
        ],
        in_specs=[vm, vm, vm, vm, anywhere, anywhere],
        out_specs=[vm, vm, anywhere, anywhere, anywhere, anywhere],
        scratch_shapes=[
            pltpu.VMEM((2, 8 * UROWS, GRP), BF),
            pltpu.VMEM((4, AREA, GRP), BF),
            pltpu.VMEM((D, 2 * FF), BF),
            pltpu.VMEM((FF, D), BF),
            pltpu.VMEM((ROWS, D), BF),
            pltpu.VMEM((D, ROWS), BF),
            pltpu.VMEM((FF, ROWS), BF),
            pltpu.VMEM((ROWS, FF), BF),
            pltpu.VMEM((ROWS, FF), F32),
            pltpu.VMEM((ROWS, FF), F32),
            pltpu.VMEM((ROWS, 2 * FF), BF),
            pltpu.VMEM((4, 384, GRP), BF),
            pltpu.VMEM((64, TOK), F32),
            pltpu.VMEM((64, TOK), F32),
            pltpu.VMEM((8, TOK), F32),
            pltpu.VMEM((GRP, GRP), BF),
            pltpu.VMEM((GRP, GRP), BF),
            pltpu.VMEM((GRP, GRP), BF),
            pltpu.VMEM((GRP, GRP), BF),
            pltpu.VMEM((128, TOK), F32),
            pltpu.VMEM((128, TOK), F32),
            pltpu.VMEM((64, TOK), F32),
            pltpu.VMEM((TOK, D), F32),
            pltpu.SemaphoreType.DMA((4, PEERS)),
            pltpu.SemaphoreType.DMA((4, PEERS)),
            pltpu.SemaphoreType.DMA((2, PEERS)),
            pltpu.SemaphoreType.DMA((2, PEERS)),
            pltpu.SemaphoreType.DMA((2, 6, 4)),
            pltpu.SemaphoreType.DMA((2, 6, 4)),
            pltpu.SemaphoreType.DMA((7,)),
            pltpu.SemaphoreType.DMA((2,)),
            pltpu.SemaphoreType.DMA((6,)),
        ],
        compiler_params=pltpu.CompilerParams(
            collective_id=0, has_side_effects=True, vmem_limit_bytes=63 * 2**20
        ),
        cost_estimate=pl.CostEstimate(
            flops=28_000_000_000, bytes_accessed=60_000_000, transcendentals=2_000_000
        ),
    )(tokens, cotangent, expert_ids.T, gate_scores.T, w_in, w_out)
    return (mixed, score_t.T, grad_in, grad_out)


def solution(mesh):
    in_specs = (
        P(("dp", "expert"), None),
        P(("dp", "expert"), None),
        P(("dp", "expert"), None),
        P("expert", None, None),
        P("expert", None, None),
        P(("dp", "expert"), None),
    )
    out_specs = (
        P(("dp", "expert"), None),
        P(("dp", "expert"), None),
        P("expert", "dp", None),
        P("expert", None, "dp"),
    )
    return jax.shard_map(shards, mesh=mesh, in_specs=in_specs, out_specs=out_specs, check_vma=False)
```

time: 597 us -> 248 us (0.42)
  Pallas kernels: 0 us -> 234 us
  waiting for transfers between devices: 180 us -> 0 us
  blocking collectives: 136 us -> 0 us
  local copies, waits for them, and re-layouts: 112 us -> 8.17 us
  matrix products: 97.3 us -> 0 us
  other arithmetic: 41.8 us -> 0 us
  between operations: 14.6 us -> 0.65 us
  starting transfers between devices: 7.47 us -> 0 us
    pallas_call x0 -> x1, Pallas kernels: none -> 234 us  [shards(): pl.pallas_call(kernel, out_shape=[jax.ShapeDtypeStruct((TOK, D), BF), jax...]
    all_to_all x2 -> x0, blocking collectives: 136 us -> none  [the longest x1 68.2 us: shards(): lax.all_to_all(grad_send, 'expert', split_axis=0, concat_axis=0, tiled=True)]
    reduce_scatter x2 -> x0, waiting for transfers between devices: 122 us -> none  [the longest x1 117 us: shards(): lax.psum_scatter(term_in.astype(jnp.bfloat16), 'dp', scatter_dimension=1,...]
    dot_general x6 -> x0, matrix products: 97.3 us -> none  [the longest x1 35.2 us: shards(): jnp.einsum('nemd,nemf->edf', received, gu_grad, preferred_element_type=jn...]
    all_to_all x1 -> x0, waiting for transfers between devices: 57.6 us -> none  [shards(): lax.all_to_all(produced, 'expert', split_axis=0, concat_axis=0, tiled=True)]
    gather x5 -> x0, local copies, waits for them, and re-layouts: 49.7 us -> none  [the longest x2 22.5 us: shards(): scaled[safe]]
    select_n x2 -> x0, local copies, waits for them, and re-layouts: 22.1 us -> none  [the longest x1 11 us: shards(): rows_in = jnp.where(valid[:, None], tokens[safe // topk], zero_bf)]
    another operation x4 -> x0, other arithmetic: 19.4 us -> none
  transfers between devices with their start and end apart: 3 -> 0, of which waited for: 3 -> 0; matrix products, arithmetic and copies ran while one was open for 10% -> 0% of each run, Pallas kernels for 0% -> 0%
where the time goes in v1:
time: 248 us; the launch traced here: 243 us
  Pallas kernels  234 us (94%)
  local copies, waits for them, and re-layouts  8.17 us (3%)
    pallas_call x1, Pallas kernels, shards(): pl.pallas_call(kernel, out_shape=[jax.ShapeDtypeStruct((TOK, D), BF), jax...  234 us
    unnamed x6, local copies, waits for them, and re-layouts  8.17 us

profile of v1, /device:TPU:57, one launch (start us, length us, event | category | flops | bytes accessed | tf_op | source)
XLA Modules:
  0.0 243.0 jit_solution(8570890353656816480)
XLA Ops:
  0.6 234.2 %shard_map.93 = (bf16[128,2048]{1,0:T(8,128)(2,1)}, f32[8,128]{1,0:T(8,128)}, bf16[2,512,1536]{2,1,0:T(8,128)(2,1)}, bf16[2,768,512]{2,1,0:T(8,128)(2,1)}, bf16[...) custom-call(bf16[128,2048]{1,0:T(8,128)(2,1)} %tok.1, bf16[128,2048]{1,0:T(8,128)(2,1)} %cot.1, s32[8,128]{1,0:T(8,128)} %bitcast.4, ...), custom_call_target="tpu_custom_call" | custom-call | flops 28000000000 | bytes 60000000 | tf_op jit(solution)/shard_map/pallas_call | solution.py:501
  234.9 0.0 copy-start
  234.9 2.0 copy.14
  236.9 1.3 copy.15
  238.1 3.8 %copy.16 = bf16[2,512,1536]{2,1,0:T(8,128)(2,1)} copy(bf16[2,512,1536]{2,1,0:T(8,128)(2,1)} %get-tuple-element.18) | data formatting | bytes 6291456
  241.9 0.0 copy-done
  241.9 1.1 copy.17
Async XLA Ops:
  234.9 7.0 %copy-start = (bf16[2,768,512]{2,1,0:T(8,128)(2,1)S(1)}, bf16[2,768,512]{2,1,0:T(8,128)(2,1)}, u32[]{:S(2)}) copy-start(bf16[2,768,512]{2,1,0:T(8,128)(2,1)} %get-tuple-element.19) | copy-start | bytes 4718596

commit v2 on v1

--- a/solution.py
+++ b/solution.py
@@ -38,8 +38,19 @@
     return lax.rem(y + dy, 4) * 8 + lax.rem(x + dx, 4) * 2 + lax.rem(c + dc, 2)
 
 
-def turn(me, i):
-    return peer(me, lax.rem(i * 11, PEERS))
+def chip(me, n, sign):
+    k = lax.rem(n * 7, BATCH)
+    x = lax.rem(lax.div(me, 2), 4) + 4 + sign * lax.rem(k, 4)
+    y = lax.div(me, 8) + 4 + sign * lax.div(k, 4)
+    return lax.rem(y, 4) * 4 + lax.rem(x, 4)
+
+
+def target(me, n, core):
+    return 2 * chip(me, n, 1) + core
+
+
+def source_of(me, i):
+    return 2 * chip(me, lax.div(i, 2), -1) + lax.rem(i, 2)
 
 
 def iota(shape, dim):
@@ -110,13 +121,16 @@
     main_slot = iota((MAIN, TOK), 0).astype(F32)
     over_row = iota((MAIN, TOK), 0)
     over_slot = (16 + lax.rem(over_row, 4)).astype(F32)
-    over_group = lax.div(over_row, 4)
+    group = lax.rem(lax.div(iota((BATCH * MAIN, TOK), 0), 4), 4)
 
     def block(q):
         return pl.ds(pl.multiple_of(q * BLK, 16), BLK)
 
+    def send_row(a, q):
+        return lax.rem(q, 2) * AREA + a * (AREA // 2) + lax.div(q, 2) * BLK
+
     def send_block(j, a, q):
-        return big.at[j, pl.ds(pl.multiple_of(a * AREA + q * BLK, 16), BLK)]
+        return big.at[j, pl.ds(pl.multiple_of(send_row(a, q), 16), BLK)]
 
     def dispatch_copy(j, a, q, lands):
         return pltpu.make_async_remote_copy(
@@ -133,72 +147,81 @@
             send_block(j, a, me), recv.at[2 * j + a, block(me)], l_sem.at[2 * j + a]
         )
 
-    def dispatch(j, a):
+    def make(j, a, core):
         source = (tok, cot)[a]
-
-        def batch(g, _):
-            hots, overs, w_main, w_over = [], [], [], []
+        hots, overs, w_main, w_over = [], [], [], []
+        for u in range(BATCH):
+            q = target(me, u, core)
+            mine = slot[pl.ds(j * PEERS + q, 1), :]
+            hot = jnp.where(main_slot == mine, 1.0, 0.0)
+            hot4 = jnp.where(over_slot == mine, 1.0, 0.0)
+            hots.append(hot)
+            overs.append(hot4)
+            if a == 1:
+                heavy = wgt[pl.ds(j * PEERS + q, 1), :]
+                w_main.append(jnp.sum(hot * heavy, axis=1, keepdims=True))
+                w_over.append(jnp.sum(hot4 * heavy, axis=1, keepdims=True))
+        pick = jnp.concatenate(hots, axis=0).astype(BF)
+        pick4 = jnp.concatenate(overs, axis=0)
+        scale = jnp.concatenate(w_main, axis=0) if a == 1 else None
+        scale4 = jnp.concatenate(w_over, axis=0) if a == 1 else None
+        extra = None
+        for c in range(4):
+            columns = source[:, c * GRP : (c + 1) * GRP]
+            rows = dot(pick, columns)
+            more = dot(jnp.where(group == c, pick4, 0.0).astype(BF), columns)
+            extra = more if extra is None else extra + more
+            if a == 1:
+                rows = rows * scale
+            rows = rows.astype(BF)
             for u in range(BATCH):
-                q = turn(me, g * BATCH + u)
-                mine = slot[pl.ds(j * PEERS + q, 1), :]
-                hot = jnp.where(main_slot == mine, 1.0, 0.0)
-                hot4 = jnp.where(over_slot == mine, 1.0, 0.0)
-                hots.append(hot)
-                overs.append(
-                    jnp.concatenate(
-                        [jnp.where(over_group == c, hot4, 0.0) for c in range(4)], axis=1
-                    )
-                )
-                if a == 1:
-                    heavy = wgt[pl.ds(j * PEERS + q, 1), :]
-                    w_main.append(jnp.sum(hot * heavy, axis=1, keepdims=True))
-                    w_over.append(jnp.sum(hot4 * heavy, axis=1, keepdims=True))
-            pick = jnp.concatenate(hots, axis=0).astype(BF)
-            pick4 = jnp.concatenate(overs, axis=0).astype(BF)
-            scale = jnp.concatenate(w_main, axis=0) if a == 1 else None
-            scale4 = jnp.concatenate(w_over, axis=0) if a == 1 else None
-            extra = None
-            for c in range(4):
-                columns = source[:, c * GRP : (c + 1) * GRP]
-                rows = dot(pick, columns)
-                more = dot(pick4[:, c * TOK : (c + 1) * TOK], columns)
-                extra = more if extra is None else extra + more
-                if a == 1:
-                    rows = rows * scale
-                rows = rows.astype(BF)
-                for u in range(BATCH):
-                    q = turn(me, g * BATCH + u)
-                    at = pl.multiple_of(a * AREA + q * BLK + 16 * c, 16)
-                    big[j, pl.ds(at, 16), :] = rows[u * 16 : u * 16 + 16, :]
-            if a == 1:
-                extra = extra * scale4
-            extra = extra.astype(BF)
-            for u in range(BATCH):
-                q = turn(me, g * BATCH + u)
-                at = pl.multiple_of(a * AREA + q * BLK + 64, 16)
-                big[j, pl.ds(at, 16), :] = extra[u * 16 : u * 16 + 16, :]
-
-            def go(i, _):
-                q = turn(me, i)
-
-                @pl.when(i > 0)
+                at = pl.multiple_of(send_row(a, target(me, u, core)) + 16 * c, 16)
+                big[j, pl.ds(at, 16), :] = rows[u * 16 : u * 16 + 16, :]
+        if a == 1:
+            extra = extra * scale4
+        extra = extra.astype(BF)
+        for u in range(BATCH):
+            at = pl.multiple_of(send_row(a, target(me, u, core)) + 64, 16)
+            big[j, pl.ds(at, 16), :] = extra[u * 16 : u * 16 + 16, :]
+
+    def gone(j, a, core):
+        def one(n, _):
+            q = target(me, n, core)
+
+            @pl.when(q != me)
+            def _():
+                dispatch_copy(j, a, q, me).wait_send()
+
+            return 0
+
+        lax.fori_loop(0, BATCH, one, 0)
+
+    def launch(j, a, core, after=None):
+        def go(n, _):
+            q = target(me, n, core)
+            if after is not None:
+                aj, aa, ac = after
+                before = target(me, n, ac)
+
+                @pl.when(before != me)
                 def _():
-                    dispatch_copy(j, a, q, me).start()
-
-                @pl.when(i == 0)
-                def _():
-                    own_copy(j, a).start()
-
-                return 0
-
-            lax.fori_loop(g * BATCH, (g + 1) * BATCH, go, 0)
-            return 0
-
-        lax.fori_loop(0, PEERS // BATCH, batch, 0)
+                    dispatch_copy(aj, aa, before, me).wait_send()
+
+            @pl.when(q != me)
+            def _():
+                dispatch_copy(j, a, q, me).start()
+
+            @pl.when(q == me)
+            def _():
+                own_copy(j, a).start()
+
+            return 0
+
+        lax.fori_loop(0, BATCH, go, 0)
 
     def assemble(aj, wait):
         def one(i, _):
-            q = turn(me, i)
+            q = source_of(me, i)
             if wait is not None:
                 wait(i, q)
             for c in range(4):
@@ -217,11 +240,11 @@
 
     def arrive(j, a):
         def wait(i, q):
-            @pl.when(i > 0)
+            @pl.when(q != me)
             def _():
                 dispatch_copy(j, a, q, q).wait_recv()
 
-            @pl.when(i == 0)
+            @pl.when(q == me)
             def _():
                 own_copy(j, a).wait()
 
@@ -242,6 +265,8 @@
 
     def forward(j):
         arrive(j, 0)
+        if j == 0:
+            pl.when(core == 1)(second)
 
         def flip(c, _):
             at = pl.ds(pl.multiple_of(c * GRP, GRP), GRP)
@@ -281,61 +306,65 @@
         for q in range(PEERS):
             recv[2 * j, q * BLK + 64 : q * BLK + 80, :] = moved[16 * q : 16 * q + 16, :]
 
+    def send_back(j):
         def go(i, _):
-            return_copy(j, turn(me, i), me).start()
-            return 0
-
-        lax.fori_loop(1, PEERS, go, 0)
+            q = source_of(me, i)
+
+            @pl.when(q != me)
+            def _():
+                return_copy(j, q, me).start()
+
+            return 0
+
+        lax.fori_loop(0, PEERS, go, 0)
         own_return(j).start()
 
     def unit_rows(u, p):
         at, n = rows_of(p)
         return pl.ds(pl.multiple_of(u * UROWS + at, 128), n)
 
+    def unit_at(j, u, p):
+        at, n = rows_of(p)
+        if u < 2:
+            buf, row = j, u * UROWS
+        elif u < 4:
+            buf, row = 1 - j, (2 * AREA if j == 0 else AREA) + (u - 2) * UROWS
+        else:
+            buf, row = j, 2 * AREA + (u - 4) * UROWS
+        return buf, pl.ds(pl.multiple_of(row + at, 128), n)
+
     def z_copy(j, k, p):
-        side_of = lax.rem(jnp.int32(k), 2) if isinstance(k, int) else lax.rem(k, 2)
-        to = jnp.where(side_of == 0, right, left)
         return pltpu.make_async_remote_copy(
-            src_ref=big.at[j, unit_rows(k, p)],
+            src_ref=big.at[unit_at(j, k, p)],
             dst_ref=parts.at[j, unit_rows(k, p)],
             send_sem=z_send.at[j, k, p],
             recv_sem=z_recv.at[j, k, p],
-            device_id=(to, me),
+            device_id=((right, left)[k % 2], me),
             device_id_type=MESH,
         )
 
-    def unit_of(u):
-        odd = lax.rem(u, 2)
-        far = jnp.where(u < 2, 2, jnp.where(u < 6, 1 + 2 * odd, 0))
-        half = jnp.where(lax.div(u, 2) == 1, 1 - odd, odd)
-        return lax.rem(b + far, 4), half
+    owners = ((2, 0, 1, (0, 1)), (1, 4, 2, (2,)), (3, 3, 5, (3,)), (0, 6, 7, ()))
+
+    def put(j, p, entry, term):
+        n = rows_of(p)[1]
+        _, first, second, leave = entry
+        for u, piece in ((first, term[0:n, :]), (second, term[n : 2 * n, :])):
+            buf, at = unit_at(j, u, p)
+            big[buf, at, :] = piece
+        for u in leave:
+            z_copy(j, u, p).start()
 
     def backward(j):
         arrive(j, 1)
 
-        def sent(i, _):
-            q = turn(me, i)
-            dispatch_copy(j, 0, q, me).wait_send()
-            dispatch_copy(j, 1, q, me).wait_send()
-            return 0
-
-        lax.fori_loop(1, PEERS, sent, 0)
-
-        def unit_out(u, _):
-            o, half = unit_of(u)
-            term = dot(
-                ht[pl.ds(pl.multiple_of(half * 384, 128), 384), :],
-                xs[:, pl.ds(pl.multiple_of(o * GRP, GRP), GRP)],
-            )
-            big[j, unit_rows(u, 0), :] = term.astype(BF)
-
-            @pl.when(u < 4)
-            def _():
-                z_copy(j, u, 0).start()
-
-            return 0
-
-        lax.fori_loop(0, 8, unit_out, 0)
+        if j == 1:
+            for a in range(2):
+                gone(0, a, 1)
+                gone(1, a, 0)
+            each(lambda j, p: [z_copy(j, k, p).wait_send() for k in (2, 3)], 0, 0, 4)
+        for entry in owners:
+            o = lax.rem(b + entry[0], 4)
+            put(j, 0, entry, dot(ht[...], xs[:, pl.ds(pl.multiple_of(o * GRP, GRP), GRP)]).astype(BF))
 
         def part(n, _):
             at = pl.ds(pl.multiple_of(n * 256, 256), 256)
@@ -350,23 +379,15 @@
         if j == 0:
             load_out(1).start()
 
-        def unit_in(i, _):
-            p = 1 + lax.div(i, 8)
-            u = lax.rem(i, 8)
-            o, half = unit_of(u)
-            term = dot(
-                xt[pl.ds(pl.multiple_of(o * GRP + half * 256, 256), 256), :],
-                gg[:, pl.ds(pl.multiple_of((p - 1) * GRP, GRP), GRP)],
-            )
-            big[j, unit_rows(u, p), :] = term.astype(BF)
-
-            @pl.when(u < 4)
-            def _():
-                z_copy(j, u, p).start()
-
-            return 0
-
-        lax.fori_loop(0, 24, unit_in, 0)
+        def unit_in(p, _):
+            columns = pl.ds(pl.multiple_of((p - 1) * GRP, GRP), GRP)
+            for entry in owners:
+                o = lax.rem(b + entry[0], 4)
+                rows = pl.ds(pl.multiple_of(o * GRP, GRP), GRP)
+                put(j, p, entry, dot(xt[rows, :], gg[:, columns]).astype(BF))
+            return 0
+
+        lax.fori_loop(1, 4, unit_in, 0)
 
     def fetch(j, k, p, where):
         n = rows_of(p)[1]
@@ -381,18 +402,17 @@
             fetch(j, d, p, d).start()
         for d in range(2):
             fetch(j, d, p, d).wait()
-            at = unit_rows(4 + d, p)
-            both = big[j, at, :].astype(F32) + stage[d, 0:n, :].astype(F32)
-            big[j, at, :] = both.astype(BF)
+            buf, at = unit_at(j, 4 + d, p)
+            both = big[buf, at, :].astype(F32) + stage[d, 0:n, :].astype(F32)
+            big[buf, at, :] = both.astype(BF)
             z_copy(j, 4 + d, p).start()
 
     def result_copy(j, h, p):
-        at, n = rows_of(p)
-        if isinstance(p, int) and p == 0:
+        if isinstance(p, int):
             to = gout.at[j, pl.ds(384 * h, 384)]
         else:
             to = gin.at[j, pl.ds(256 * h, 256), pl.ds(pl.multiple_of((p - 1) * GRP, GRP), GRP)]
-        return pltpu.make_async_copy(big.at[j, unit_rows(6 + h, p)], to, o_sem.at[4 + h])
+        return pltpu.make_async_copy(big.at[unit_at(j, 6 + h, p)], to, o_sem.at[4 + h])
 
     def finish(j, p):
         n = rows_of(p)[1]
@@ -402,13 +422,13 @@
         for h in range(2):
             fetch(j, 4 + h, p, 2 + h).wait()
             fetch(j, 3 - h, p, 1 - h).wait()
-            at = unit_rows(6 + h, p)
+            buf, at = unit_at(j, 6 + h, p)
             whole = (
-                big[j, at, :].astype(F32)
+                big[buf, at, :].astype(F32)
                 + stage[2 + h, 0:n, :].astype(F32)
                 + stage[1 - h, 0:n, :].astype(F32)
             )
-            big[j, at, :] = whole.astype(BF)
+            big[buf, at, :] = whole.astype(BF)
             result_copy(j, h, p).start()
         for h in range(2):
             result_copy(j, h, p).wait()
@@ -425,7 +445,7 @@
 
     def combine(j):
         def arrived(i, _):
-            q = turn(me, i)
+            q = peer(me, i)
             return_copy(j, q, q).wait_recv()
             return_copy(j, q, q).wait_send()
             return 0
@@ -463,17 +483,36 @@
             else:
                 mixed[:, at] = (macc[:, at] + made).astype(BF)
 
+    core = lax.rem(me, 2)
+
+    def first():
+        launch(0, 0, 1, (0, 1, 0))
+        launch(0, 1, 1)
+
+    def second():
+        for target_core in range(2):
+            for a in range(2):
+                launch(1, a, target_core)
+
+    make(0, 0, 0)
     pl.semaphore_wait(barrier, PEERS + 1)
-    dispatch(0, 0)
-    dispatch(0, 1)
-    dispatch(1, 0)
-    dispatch(1, 1)
+    launch(0, 0, 0)
+    for a, target_core in ((1, 0), (0, 1), (1, 1)):
+        make(0, a, target_core)
+    launch(0, 1, 0, (0, 0, 0))
+    for target_core in range(2):
+        for a in range(2):
+            make(1, a, target_core)
+    pl.when(core == 1)(first)
     forward(0)
+    pl.when(core == 0)(first)
     backward(0)
-    each(middle, 0, 0, 2)
+    pl.when(core == 0)(second)
+    each(middle, 0, 0, 4)
     forward(1)
-    each(middle, 0, 2, 4)
     backward(1)
+    send_back(0)
+    send_back(1)
     each(finish, 0, 0, 4)
     each(middle, 1, 0, 4)
     combine(0)
@@ -485,14 +524,18 @@
         )
     affinity = jnp.concatenate(found, axis=0)
     score[...] = (affinity - jnp.sum(weights * affinity, axis=0, keepdims=True)) / total
+
     each(finish, 1, 0, 4)
-
-    def sent(j, p):
+    for a in range(2):
+        gone(1, a, 1)
+
+    def last(j, p):
         for k in range(6):
-            z_copy(j, k, p).wait_send()
-
-    each(sent, 0, 0, 4)
-    each(sent, 1, 0, 4)
+            if j == 1 or k not in (2, 3):
+                z_copy(j, k, p).wait_send()
+
+    each(last, 0, 0, 4)
+    each(last, 1, 0, 4)
 
 
 def shards(tokens, expert_ids, gate_scores, w_in, w_out, cotangent):
@@ -511,7 +554,7 @@
         in_specs=[vm, vm, vm, vm, anywhere, anywhere],
         out_specs=[vm, vm, anywhere, anywhere, anywhere, anywhere],
         scratch_shapes=[
-            pltpu.VMEM((2, 8 * UROWS, GRP), BF),
+            pltpu.VMEM((2, 2 * AREA + 4 * UROWS, GRP), BF),
             pltpu.VMEM((4, AREA, GRP), BF),
             pltpu.VMEM((D, 2 * FF), BF),
             pltpu.VMEM((FF, D), BF),

time: 248 us -> 222 us (0.90)
  the two profiles are of different devices: /device:TPU:57 before, /device:TPU:29 now
where the time goes in v2:
time: 222 us
  Pallas kernels  213 us (96%)
  local copies, waits for them, and re-layouts  8.17 us (4%)
    pallas_call x1, Pallas kernels, shards(): pl.pallas_call(kernel, out_shape=[jax.ShapeDtypeStruct((TOK, D), BF), jax...  213 us
    unnamed x6, local copies, waits for them, and re-layouts  8.17 us

profile of v2, /device:TPU:29, one launch (start us, length us, event | category | flops | bytes accessed | tf_op | source)
XLA Modules:
  0.0 221.5 jit_solution(17138302746415491669)
XLA Ops:
  0.6 212.7 %shard_map.93 = (bf16[128,2048]{1,0:T(8,128)(2,1)}, f32[8,128]{1,0:T(8,128)}, bf16[2,512,1536]{2,1,0:T(8,128)(2,1)}, bf16[2,768,512]{2,1,0:T(8,128)(2,1)}, bf16[...) custom-call(bf16[128,2048]{1,0:T(8,128)(2,1)} %tok.1, bf16[128,2048]{1,0:T(8,128)(2,1)} %cot.1, s32[8,128]{1,0:T(8,128)} %bitcast.4, ...), custom_call_target="tpu_custom_call" | custom-call | flops 28000000000 | bytes 60000000 | tf_op jit(solution)/shard_map/pallas_call | solution.py:544
  213.4 0.0 copy-start
  213.4 2.0 copy.14
  215.4 1.3 copy.15
  216.6 3.8 %copy.16 = bf16[2,512,1536]{2,1,0:T(8,128)(2,1)} copy(bf16[2,512,1536]{2,1,0:T(8,128)(2,1)} %get-tuple-element.18) | data formatting | bytes 6291456
  220.4 0.0 copy-done
  220.4 1.1 copy.17
Async XLA Ops:
  213.4 7.0 %copy-start = (bf16[2,768,512]{2,1,0:T(8,128)(2,1)S(1)}, bf16[2,768,512]{2,1,0:T(8,128)(2,1)}, u32[]{:S(2)}) copy-start(bf16[2,768,512]{2,1,0:T(8,128)(2,1)} %get-tuple-element.19) | copy-start | bytes 4718596

commit v3 on v2

--- a/solution.py
+++ b/solution.py
@@ -68,7 +68,7 @@
     mixed, score, gin, gout, back, parts,
     big, recv, win, wout, xs, xt, ht, hid, gate, up, gg, stage, slot, wgt, cut, perm, perm_t,
     over, side, slot4, wgt4, aff, macc,
-    d_send, d_recv, r_send, r_recv, z_send, z_recv, l_sem, w_sem, o_sem,
+    d_send, d_recv, r_send, r_recv, z_send, z_recv, l_sem, w_sem, o_sem, g_sem, b_sem,
 ):
     b = lax.axis_index("dp")
     me = lax.axis_index("expert")
@@ -407,31 +407,35 @@
             big[buf, at, :] = both.astype(BF)
             z_copy(j, 4 + d, p).start()
 
+    def early(j, p):
+        n = rows_of(p)[1]
+        for k in (3, 2):
+            z_copy(j, k, p).wait_recv()
+            fetch(j, k, p, k).start()
+        for h in range(2):
+            fetch(j, 3 - h, p, 3 - h).wait()
+            buf, at = unit_at(j, 6 + h, p)
+            both = big[buf, at, :].astype(F32) + stage[3 - h, 0:n, :].astype(F32)
+            big[buf, at, :] = both.astype(BF)
+
     def result_copy(j, h, p):
         if isinstance(p, int):
             to = gout.at[j, pl.ds(384 * h, 384)]
         else:
             to = gin.at[j, pl.ds(256 * h, 256), pl.ds(pl.multiple_of((p - 1) * GRP, GRP), GRP)]
-        return pltpu.make_async_copy(big.at[unit_at(j, 6 + h, p)], to, o_sem.at[4 + h])
+        return pltpu.make_async_copy(big.at[unit_at(j, 6 + h, p)], to, g_sem.at[j, h, p])
 
     def finish(j, p):
         n = rows_of(p)[1]
-        for k in (3, 2, 4, 5):
-            z_copy(j, k, p).wait_recv()
-            fetch(j, k, p, k - 2).start()
         for h in range(2):
-            fetch(j, 4 + h, p, 2 + h).wait()
-            fetch(j, 3 - h, p, 1 - h).wait()
+            z_copy(j, 4 + h, p).wait_recv()
+            fetch(j, 4 + h, p, h).start()
+        for h in range(2):
+            fetch(j, 4 + h, p, h).wait()
             buf, at = unit_at(j, 6 + h, p)
-            whole = (
-                big[buf, at, :].astype(F32)
-                + stage[2 + h, 0:n, :].astype(F32)
-                + stage[1 - h, 0:n, :].astype(F32)
-            )
+            whole = big[buf, at, :].astype(F32) + stage[h, 0:n, :].astype(F32)
             big[buf, at, :] = whole.astype(BF)
             result_copy(j, h, p).start()
-        for h in range(2):
-            result_copy(j, h, p).wait()
 
     def each(fn, j, lo, hi):
         if lo == 0:
@@ -444,18 +448,22 @@
         lax.fori_loop(max(lo, 1), hi, one, 0)
 
     def combine(j):
+        def take(q):
+            return pltpu.make_async_copy(
+                back.at[j, block(q)], recv.at[2 * j + 1, block(q)], b_sem.at[q]
+            )
+
+        own_return(j).wait()
+        take(me).start()
+
         def arrived(i, _):
             q = peer(me, i)
             return_copy(j, q, q).wait_recv()
-            return_copy(j, q, q).wait_send()
+            take(q).start()
             return 0
 
         lax.fori_loop(1, PEERS, arrived, 0)
-        own_return(j).wait()
-        whole = pltpu.make_async_copy(back.at[j], recv.at[2 * j + 1], l_sem.at[6])
-        whole.start()
-        whole.wait()
-        assemble(2 * j + 1, None)
+        assemble(2 * j + 1, lambda i, q: take(q).wait())
         mine = slot[j * PEERS : (j + 1) * PEERS, :]
         heavy = wgt[j * PEERS : (j + 1) * PEERS, :]
         for s in range(4):
@@ -513,9 +521,16 @@
     backward(1)
     send_back(0)
     send_back(1)
-    each(finish, 0, 0, 4)
-    each(middle, 1, 0, 4)
+
+    def between(j, p):
+        middle(1, p)
+        early(0, p)
+        finish(0, p)
+
+    each(between, 0, 0, 4)
+    each(early, 1, 0, 4)
     combine(0)
+    each(finish, 1, 0, 2)
     combine(1)
     found = []
     for k in range(8):
@@ -525,14 +540,24 @@
     affinity = jnp.concatenate(found, axis=0)
     score[...] = (affinity - jnp.sum(weights * affinity, axis=0, keepdims=True)) / total
 
-    each(finish, 1, 0, 4)
+    each(finish, 1, 2, 4)
     for a in range(2):
         gone(1, a, 1)
+
+    def returned(i, _):
+        q = peer(me, i)
+        for j in range(2):
+            return_copy(j, q, q).wait_send()
+        return 0
+
+    lax.fori_loop(1, PEERS, returned, 0)
 
     def last(j, p):
         for k in range(6):
             if j == 1 or k not in (2, 3):
                 z_copy(j, k, p).wait_send()
+        for h in range(2):
+            result_copy(j, h, p).wait()
 
     each(last, 0, 0, 4)
     each(last, 1, 0, 4)
@@ -585,7 +610,9 @@
             pltpu.SemaphoreType.DMA((2, 6, 4)),
             pltpu.SemaphoreType.DMA((7,)),
             pltpu.SemaphoreType.DMA((2,)),
-            pltpu.SemaphoreType.DMA((6,)),
+            pltpu.SemaphoreType.DMA((4,)),
+            pltpu.SemaphoreType.DMA((2, 2, 4)),
+            pltpu.SemaphoreType.DMA((PEERS,)),
         ],
         compiler_params=pltpu.CompilerParams(
             collective_id=0, has_side_effects=True, vmem_limit_bytes=63 * 2**20

time: 222 us -> 220 us (level)
  the two profiles are of different devices: /device:TPU:29 before, /device:TPU:57 now
where the time goes in v3:
time: 220 us; the launch traced here: 217 us
  Pallas kernels  208 us (95%)
  local copies, waits for them, and re-layouts  8.17 us (4%)
    pallas_call x1, Pallas kernels, shards(): pl.pallas_call(kernel, out_shape=[jax.ShapeDtypeStruct((TOK, D), BF), jax...  208 us
    unnamed x6, local copies, waits for them, and re-layouts  8.17 us

profile of v3, /device:TPU:57, one launch (start us, length us, event | category | flops | bytes accessed | tf_op | source)
XLA Modules:
  0.0 216.9 jit_solution(3738365967350921451)
XLA Ops:
  0.6 208.1 %shard_map.93 = (bf16[128,2048]{1,0:T(8,128)(2,1)}, f32[8,128]{1,0:T(8,128)}, bf16[2,512,1536]{2,1,0:T(8,128)(2,1)}, bf16[2,768,512]{2,1,0:T(8,128)(2,1)}, bf16[...) custom-call(bf16[128,2048]{1,0:T(8,128)(2,1)} %tok.1, bf16[128,2048]{1,0:T(8,128)(2,1)} %cot.1, s32[8,128]{1,0:T(8,128)} %bitcast.4, ...), custom_call_target="tpu_custom_call" | custom-call | flops 28000000000 | bytes 60000000 | tf_op jit(solution)/shard_map/pallas_call | solution.py:569
  208.7 0.0 copy-start
  208.7 2.0 copy.14
  210.7 1.3 copy.15
  212.0 3.8 %copy.16 = bf16[2,512,1536]{2,1,0:T(8,128)(2,1)} copy(bf16[2,512,1536]{2,1,0:T(8,128)(2,1)} %get-tuple-element.18) | data formatting | bytes 6291456
  215.7 0.0 copy-done
  215.7 1.1 copy.17
Async XLA Ops:
  208.7 7.0 %copy-start = (bf16[2,768,512]{2,1,0:T(8,128)(2,1)S(1)}, bf16[2,768,512]{2,1,0:T(8,128)(2,1)}, u32[]{:S(2)}) copy-start(bf16[2,768,512]{2,1,0:T(8,128)(2,1)} %get-tuple-element.19) | copy-start | bytes 4718596

commit v4 on v3

--- a/solution.py
+++ b/solution.py
@@ -108,15 +108,6 @@
     earlier = jnp.where(iota((TOK, TOK), 0) < iota((TOK, TOK), 1), 1.0, 0.0).astype(BF)
     slot[...] = jnp.where(member > 0.0, dot(member.astype(BF), earlier), -1.0)
     wgt[...] = weight
-
-    r0, r1 = iota((GRP, GRP), 0), iota((GRP, GRP), 1)
-
-    def place(m):
-        r = lax.rem(m, 128)
-        return 16 * lax.div(r, 4) + 4 * lax.div(m, 128) + lax.rem(r, 4)
-
-    perm[...] = jnp.where(r1 == place(r0), 1.0, 0.0).astype(BF)
-    perm_t[...] = jnp.where(r0 == place(r1), 1.0, 0.0).astype(BF)
 
     main_slot = iota((MAIN, TOK), 0).astype(F32)
     over_row = iota((MAIN, TOK), 0)
@@ -365,6 +356,8 @@
         for entry in owners:
             o = lax.rem(b + entry[0], 4)
             put(j, 0, entry, dot(ht[...], xs[:, pl.ds(pl.multiple_of(o * GRP, GRP), GRP)]).astype(BF))
+            if j == 0 and entry[0] == 2:
+                pl.when(core == 0)(first_grads)
 
         def part(n, _):
             at = pl.ds(pl.multiple_of(n * 256, 256), 256)
@@ -495,6 +488,8 @@
 
     def first():
         launch(0, 0, 1, (0, 1, 0))
+
+    def first_grads():
         launch(0, 1, 1)
 
     def second():
@@ -505,13 +500,25 @@
     make(0, 0, 0)
     pl.semaphore_wait(barrier, PEERS + 1)
     launch(0, 0, 0)
-    for a, target_core in ((1, 0), (0, 1), (1, 1)):
-        make(0, a, target_core)
-    launch(0, 1, 0, (0, 0, 0))
+    make(0, 1, 0)
+
+    r0, r1 = iota((GRP, GRP), 0), iota((GRP, GRP), 1)
+
+    def place(m):
+        r = lax.rem(m, 128)
+        return 16 * lax.div(r, 4) + 4 * lax.div(m, 128) + lax.rem(r, 4)
+
+    perm[...] = jnp.where(r1 == place(r0), 1.0, 0.0).astype(BF)
+    perm_t[...] = jnp.where(r0 == place(r1), 1.0, 0.0).astype(BF)
+
+    for a in range(2):
+        make(0, a, 1)
     for target_core in range(2):
         for a in range(2):
             make(1, a, target_core)
+    launch(0, 1, 0, (0, 0, 0))
     pl.when(core == 1)(first)
+    pl.when(core == 1)(first_grads)
     forward(0)
     pl.when(core == 0)(first)
     backward(0)

time: 220 us -> 229 us (1.041); the launches traced: 217 us -> 228 us
  Pallas kernels: 208 us -> 220 us
    pallas_call x1, Pallas kernels: 208 us -> 220 us  [shards(): pl.pallas_call(kernel, out_shape=[jax.ShapeDtypeStruct((TOK, D), BF), jax...]
where the time goes in v4:
time: 229 us; the launch traced here: 228 us
  Pallas kernels  220 us (96%)
  local copies, waits for them, and re-layouts  8.17 us (4%)
    pallas_call x1, Pallas kernels, shards(): pl.pallas_call(kernel, out_shape=[jax.ShapeDtypeStruct((TOK, D), BF), jax...  220 us
    unnamed x6, local copies, waits for them, and re-layouts  8.17 us

profile of v4, /device:TPU:57, one launch (start us, length us, event | category | flops | bytes accessed | tf_op | source)
XLA Modules:
  0.0 228.4 jit_solution(4556513647566154849)
XLA Ops:
  0.6 219.6 %shard_map.93 = (bf16[128,2048]{1,0:T(8,128)(2,1)}, f32[8,128]{1,0:T(8,128)}, bf16[2,512,1536]{2,1,0:T(8,128)(2,1)}, bf16[2,768,512]{2,1,0:T(8,128)(2,1)}, bf16[...) custom-call(bf16[128,2048]{1,0:T(8,128)(2,1)} %tok.1, bf16[128,2048]{1,0:T(8,128)(2,1)} %cot.1, s32[8,128]{1,0:T(8,128)} %bitcast.4, ...), custom_call_target="tpu_custom_call" | custom-call | flops 28000000000 | bytes 60000000 | tf_op jit(solution)/shard_map/pallas_call | solution.py:576
  220.3 0.0 copy-start
  220.3 2.0 copy.14
  222.3 1.3 copy.15
  223.5 3.8 %copy.16 = bf16[2,512,1536]{2,1,0:T(8,128)(2,1)} copy(bf16[2,512,1536]{2,1,0:T(8,128)(2,1)} %get-tuple-element.18) | data formatting | bytes 6291456
  227.3 0.0 copy-done
  227.3 1.1 copy.17
Async XLA Ops:
  220.3 7.0 %copy-start = (bf16[2,768,512]{2,1,0:T(8,128)(2,1)S(1)}, bf16[2,768,512]{2,1,0:T(8,128)(2,1)}, u32[]{:S(2)}) copy-start(bf16[2,768,512]{2,1,0:T(8,128)(2,1)} %get-tuple-element.19) | copy-start | bytes 4718596

commit v5 on v3

--- a/solution.py
+++ b/solution.py
@@ -508,13 +508,18 @@
     for a, target_core in ((1, 0), (0, 1), (1, 1)):
         make(0, a, target_core)
     launch(0, 1, 0, (0, 0, 0))
-    for target_core in range(2):
-        for a in range(2):
-            make(1, a, target_core)
+
+    def second_blocks():
+        for target_core in range(2):
+            for a in range(2):
+                make(1, a, target_core)
+
     pl.when(core == 1)(first)
+    pl.when(core == 1)(second_blocks)
     forward(0)
     pl.when(core == 0)(first)
     backward(0)
+    pl.when(core == 0)(second_blocks)
     pl.when(core == 0)(second)
     each(middle, 0, 0, 4)
     forward(1)

time: 220 us -> 230 us (1.045); the launches traced: 217 us -> 229 us
  Pallas kernels: 208 us -> 220 us
    pallas_call x1, Pallas kernels: 208 us -> 220 us  [shards(): pl.pallas_call(kernel, out_shape=[jax.ShapeDtypeStruct((TOK, D), BF), jax...]
where the time goes in v5:
time: 230 us; the launch traced here: 229 us
  Pallas kernels  220 us (96%)
  local copies, waits for them, and re-layouts  8.17 us (4%)
    pallas_call x1, Pallas kernels, shards(): pl.pallas_call(kernel, out_shape=[jax.ShapeDtypeStruct((TOK, D), BF), jax...  220 us
    unnamed x6, local copies, waits for them, and re-layouts  8.17 us

profile of v5, /device:TPU:57, one launch (start us, length us, event | category | flops | bytes accessed | tf_op | source)
XLA Modules:
  0.0 229.3 jit_solution(4032399846891619386)
XLA Ops:
  0.6 220.5 %shard_map.93 = (bf16[128,2048]{1,0:T(8,128)(2,1)}, f32[8,128]{1,0:T(8,128)}, bf16[2,512,1536]{2,1,0:T(8,128)(2,1)}, bf16[2,768,512]{2,1,0:T(8,128)(2,1)}, bf16[...) custom-call(bf16[128,2048]{1,0:T(8,128)(2,1)} %tok.1, bf16[128,2048]{1,0:T(8,128)(2,1)} %cot.1, s32[8,128]{1,0:T(8,128)} %bitcast.4, ...), custom_call_target="tpu_custom_call" | custom-call | flops 28000000000 | bytes 60000000 | tf_op jit(solution)/shard_map/pallas_call | solution.py:574
  221.1 0.0 copy-start
  221.1 2.0 copy.14
  223.1 1.3 copy.15
  224.4 3.8 %copy.16 = bf16[2,512,1536]{2,1,0:T(8,128)(2,1)} copy(bf16[2,512,1536]{2,1,0:T(8,128)(2,1)} %get-tuple-element.18) | data formatting | bytes 6291456
  228.1 0.0 copy-done
  228.2 1.1 copy.17
Async XLA Ops:
  221.1 7.0 %copy-start = (bf16[2,768,512]{2,1,0:T(8,128)(2,1)S(1)}, bf16[2,768,512]{2,1,0:T(8,128)(2,1)}, u32[]{:S(2)}) copy-start(bf16[2,768,512]{2,1,0:T(8,128)(2,1)} %get-tuple-element.19) | copy-start | bytes 4718596
